TPU v7x, 512 devices: a whole 4x8x8 slice. The times are simulated.
512 devices in a mesh: dp: 64 (over x, z, core), section: 8 (over y).
Axes of the slice: x: 4, y: 8, z: 8, core: 2. Of those that a mesh axis runs over, the one named last changes fastest.
Arguments:
- layer_input: bfloat16 [8, 64, 128, 4096], P('section', 'dp'), may hold values from -6 to 6
- keys: bfloat16 [8, 64, 128, 512], P('section', 'dp'), may hold values from -6 to 6
- values: bfloat16 [8, 64, 128, 512], P('section', 'dp'), may hold values from -6 to 6
- top_grad: bfloat16 [64, 128, 4096], P('dp'), may hold values from -6 to 6
- gains: float32 [8, 4096], P('section'), may hold values from 0.25 to 1.75
- biases: float32 [8, 4096], P('section'), may hold values from -4 to 4
- lengths: int32 [64], P('dp'), may hold values from 1 to 128, 5120 in all
Outputs:
- grad_in: bfloat16 [8, 64, 128, 4096], P('section', 'dp')
- key_grad: float32 [8, 64, 128, 512], P('section', 'dp')
- value_grad: float32 [8, 64, 128, 512], P('section', 'dp')
- gain_grad: float32 [8, 4096], P('section', 'dp')
- bias_grad: float32 [8, 4096], P('section', 'dp')
Inputs may be any that keep to these rules, and one draw needn't show every extreme that they name: `lengths`: valid tokens of each request; some request has exactly 128.
All inputs are finite; a program needn't handle non-finite values. No bound on the sum of `lengths` on one device may be relied on, other than what follows from the above.
Results may differ from a plain program's by a relative error of at most 0.012.
Values may be sent and summed in bfloat16 or wider, within the bound.
A program may use at most 128 MiB of HBM per device.

v0:
```python
import jax
import jax.numpy as jnp
from jax import lax
from jax.sharding import PartitionSpec as P

KVH = 4
HD = 128
SPANS = 8
GROUP = 8


def shifted(array, axis, by):
    devices = lax.axis_size(axis)
    pairs = [(i, i + by) for i in range(devices) if 0 <= i + by < devices]
    return lax.ppermute(array, axis, pairs)


def mixed(form, left, right):
    return jnp.einsum(form, left, right, preferred_element_type=jnp.float32)


def block_grad(upstream, start, layer_rows, key_rows, value_rows, gain, bias, length):
    count = upstream.shape[0]
    seqlen = key_rows.shape[0]
    inputs = lax.dynamic_slice_in_dim(layer_rows, start, count, 0).astype(jnp.float32)
    inverse = lax.rsqrt(jnp.mean(inputs * inputs, -1, keepdims=True) + 1e-06)
    normed = inputs * inverse
    query = (normed * gain + bias).astype(jnp.bfloat16)
    query_heads = query.reshape(count, KVH, GROUP, HD)
    key_heads = key_rows.reshape(seqlen, KVH, HD)
    value_heads = value_rows.reshape(seqlen, KVH, HD)
    factor = HD ** (-0.5)
    scores = mixed("ikgd,jkd->kgij", query_heads, key_heads) * factor
    positions = start + jnp.arange(count, dtype=jnp.int32)
    columns = jnp.arange(seqlen, dtype=jnp.int32)
    allowed = (columns[None, :] <= positions[:, None]) & (columns[None, :] < length)
    scores = jnp.where(allowed, scores, -1e30)
    peak = jnp.max(scores, -1, keepdims=True)
    weights = jnp.exp(scores - peak)
    weights = weights / jnp.sum(weights, -1, keepdims=True)
    live = positions < length
    weights = weights * live[:, None].astype(jnp.float32)
    grad_out = jnp.where(live[:, None], upstream, jnp.zeros_like(upstream))
    grad_heads = grad_out.reshape(count, KVH, GROUP, HD)
    grad_probs = mixed("ikgd,jkd->kgij", grad_heads, value_heads)
    centre = jnp.sum(weights * grad_probs, -1, keepdims=True)
    grad_scores = (weights * (grad_probs - centre) * factor).astype(jnp.bfloat16)
    grad_query = mixed("kgij,jkd->ikgd", grad_scores, key_heads).reshape(count, -1)
    key_part = mixed("kgij,ikgd->jkd", grad_scores, query_heads).reshape(seqlen, -1)
    value_part = mixed("kgij,ikgd->jkd", weights.astype(jnp.bfloat16), grad_heads).reshape(
        seqlen, -1
    )
    bias_part = jnp.sum(grad_query, 0)
    gain_part = jnp.sum(grad_query * normed, 0)
    scaled = grad_query * gain
    grad_inputs = inverse * (scaled - normed * jnp.mean(scaled * normed, -1, keepdims=True))
    result = (upstream.astype(jnp.float32) + grad_inputs).astype(jnp.bfloat16)
    return (result, key_part, value_part, gain_part, bias_part)


def local(layer_input, keys, values, top_grad, gains, biases, lengths):
    rows_in = layer_input[0, 0]
    key_rows = keys[0, 0]
    value_rows = values[0, 0]
    top_rows = top_grad[0]
    gain = gains[0]
    bias = biases[0]
    length = lengths[0]
    sections = lax.axis_size("section")
    section_id = lax.axis_index("section")
    seqlen, width = rows_in.shape
    kv_width = key_rows.shape[1]

    def run_block(upstream, start):
        return block_grad(upstream, start, rows_in, key_rows, value_rows, gain, bias, length)

    def skip_block(upstream, start):
        return (
            jnp.zeros((upstream.shape[0], width), jnp.bfloat16),
            jnp.zeros((seqlen, kv_width), jnp.float32),
            jnp.zeros((seqlen, kv_width), jnp.float32),
            jnp.zeros((width,), jnp.float32),
            jnp.zeros((width,), jnp.float32),
        )

    grad_rows = jnp.zeros((seqlen, width), jnp.bfloat16)
    key_total = jnp.zeros((seqlen, kv_width), jnp.float32)
    value_total = jnp.zeros((seqlen, kv_width), jnp.float32)
    gain_total = jnp.zeros((width,), jnp.float32)
    bias_total = jnp.zeros((width,), jnp.float32)
    block = seqlen // SPANS

    def turn_step(turn, carry):
        arrived, grad_rows, key_total, value_total, gain_total, bias_total = carry
        offset = turn - (sections - 1 - section_id)
        active = (offset >= 0) & (offset < SPANS)
        span_id = jnp.clip(SPANS - 1 - offset, 0, SPANS - 1)
        start = span_id * block
        upstream = jnp.where(
            section_id == sections - 1, lax.dynamic_slice_in_dim(top_rows, start, block, 0), arrived
        )
        result = lax.cond(active, run_block, skip_block, upstream, start)
        current = lax.dynamic_slice_in_dim(grad_rows, start, block, 0)
        grad_rows = lax.dynamic_update_slice_in_dim(
            grad_rows, jnp.where(active, result[0], current), start, 0
        )
        arrived = shifted(result[0], "section", -1)
        return (
            arrived,
            grad_rows,
            key_total + result[1],
            value_total + result[2],
            gain_total + result[3],
            bias_total + result[4],
        )

    initial = (
        jnp.zeros((block, width), jnp.bfloat16),
        grad_rows,
        key_total,
        value_total,
        gain_total,
        bias_total,
    )
    final = lax.fori_loop(0, sections + SPANS - 1, turn_step, initial)
    grad_rows, key_total, value_total, gain_total, bias_total = (
        final[1],
        final[2],
        final[3],
        final[4],
        final[5],
    )
    gain_share, bias_share = (
        lax.psum_scatter(gain_total[None], "dp", scatter_dimension=1, tiled=True),
        lax.psum_scatter(bias_total[None], "dp", scatter_dimension=1, tiled=True),
    )
    return (
        grad_rows[None, None],
        key_total[None, None],
        value_total[None, None],
        gain_share,
        bias_share,
    )


def solution(mesh):
    return jax.shard_map(
        local,
        mesh=mesh,
        in_specs=(
            P("section", "dp", None, None),
            P("section", "dp", None, None),
            P("section", "dp", None, None),
            P("dp", None, None),
            P("section", None),
            P("section", None),
            P("dp"),
        ),
        out_specs=(
            P("section", "dp", None, None),
            P("section", "dp", None, None),
            P("section", "dp", None, None),
            P("section", "dp"),
            P("section", "dp"),
        ),
        check_vma=False,
    )
```

profile of v0, /device:TPU:1, one launch (start us, length us, event | category | flops | bytes accessed | tf_op | source)
XLA Modules:
  0.0 581.3 jit_solution(18100699622995110073)
XLA Ops:
  7.4 252.0 %while.26 = (s32[]{:T(128)}, bf16[16,4096]{1,0:T(8,128)(2,1)S(1)}, bf16[128,4096]{1,0:T(8,128)(2,1)S(1)}, f32[128,512]{0,1:T(8,128)S(1)}, f32[128,512]{0,1:T(8,1...) while((s32[]{:T(128)}, bf16[16,4096]{1,0:T(8,128)(2,1)S(1)}, ...), condition=%wide.region_10.11_spmd.clone, body=%wide.region_0.10_spmd.clone.sunk | while | flops 86784096 | bytes 9705213 | solution.py:125
  9.0 4.9 collective-permute-done
  15.5 6.1 %collective-permute-done = bf16[16,4096]{1,0:T(8,128)(2,1)S(1)} collective-permute-done((bf16[16,4096]{1,0:T(8,128)(2,1)S(1)}, bf16[16,4096]{1,0:T(8,128)(2,1)S(1)}, u32[]{:S(2)}, u32[]{:S(2)}) %collective-permute-start) | collective-permute-done | bytes 131104 | tf_op jit(solution)/shard_map/while/body/eval_jaxpr/ppermute | solution.py:15
  23.2 4.7 collective-permute-done
  29.5 4.2 collective-permute-done
  35.3 5.8 collective-permute-done
  42.7 4.7 collective-permute-done
  49.0 70.6 %collective-permute-done = bf16[16,4096]{1,0:T(8,128)(2,1)S(1)} collective-permute-done((bf16[16,4096]{1,0:T(8,128)(2,1)S(1)}, bf16[16,4096]{1,0:T(8,128)(2,1)S(1)}, u32[]{:S(2)}, u32[]{:S(2)}) %collective-permute-start) | collective-permute-done | bytes 131104 | tf_op jit(solution)/shard_map/while/body/eval_jaxpr/ppermute | solution.py:15
  119.6 10.5 %conditional.3 = (bf16[16,4096]{1,0:T(8,128)(2,1)S(1)}, f32[128,512]{0,1:T(8,128)S(1)}, f32[128,512]{0,1:T(8,128)S(1)}, f32[4096]{0:T(1024)S(1)}, f32[4096]{0:T(1024)S(1)}) conditional(s32[]{:T(128)} %convert_element_type.83, () %tuple.67, (pred[]{:T(512)}, bf16[128,4096]{1,0:T(8,128)(2,1)}, s32[]{:T(128)}, bf16[16,4096]{1,0:T(8,128)(2,1)S(1)}, ...), branch_computations={%region_1.1_spmd, %region_2.9_spmd} | conditional | flops 86440016 | bytes 7116080 | solution.py:102
  130.1 1.3 collective-permute-start
  131.6 5.8 %collective-permute-done = bf16[16,4096]{1,0:T(8,128)(2,1)S(1)} collective-permute-done((bf16[16,4096]{1,0:T(8,128)(2,1)S(1)}, bf16[16,4096]{1,0:T(8,128)(2,1)S(1)}, u32[]{:S(2)}, u32[]{:S(2)}) %collective-permute-start) | collective-permute-done | bytes 131104 | tf_op jit(solution)/shard_map/while/body/eval_jaxpr/ppermute | solution.py:15
  137.4 10.7 %conditional.3 = (bf16[16,4096]{1,0:T(8,128)(2,1)S(1)}, f32[128,512]{0,1:T(8,128)S(1)}, f32[128,512]{0,1:T(8,128)S(1)}, f32[4096]{0:T(1024)S(1)}, f32[4096]{0:T(1024)S(1)}) conditional(s32[]{:T(128)} %convert_element_type.83, () %tuple.67, (pred[]{:T(512)}, bf16[128,4096]{1,0:T(8,128)(2,1)}, s32[]{:T(128)}, bf16[16,4096]{1,0:T(8,128)(2,1)S(1)}, ...), branch_computations={%region_1.1_spmd, %region_2.9_spmd} | conditional | flops 86440016 | bytes 7116080 | solution.py:102
  148.1 1.3 collective-permute-start
  149.6 5.4 collective-permute-done
  155.0 10.7 %conditional.3 = (bf16[16,4096]{1,0:T(8,128)(2,1)S(1)}, f32[128,512]{0,1:T(8,128)S(1)}, f32[128,512]{0,1:T(8,128)S(1)}, f32[4096]{0:T(1024)S(1)}, f32[4096]{0:T(1024)S(1)}) conditional(s32[]{:T(128)} %convert_element_type.83, () %tuple.67, (pred[]{:T(512)}, bf16[128,4096]{1,0:T(8,128)(2,1)}, s32[]{:T(128)}, bf16[16,4096]{1,0:T(8,128)(2,1)S(1)}, ...), branch_computations={%region_1.1_spmd, %region_2.9_spmd} | conditional | flops 86440016 | bytes 7116080 | solution.py:102
  167.2 5.4 collective-permute-done
  172.6 10.7 %conditional.3 = (bf16[16,4096]{1,0:T(8,128)(2,1)S(1)}, f32[128,512]{0,1:T(8,128)S(1)}, f32[128,512]{0,1:T(8,128)S(1)}, f32[4096]{0:T(1024)S(1)}, f32[4096]{0:T(1024)S(1)}) conditional(s32[]{:T(128)} %convert_element_type.83, () %tuple.67, (pred[]{:T(512)}, bf16[128,4096]{1,0:T(8,128)(2,1)}, s32[]{:T(128)}, bf16[16,4096]{1,0:T(8,128)(2,1)S(1)}, ...), branch_computations={%region_1.1_spmd, %region_2.9_spmd} | conditional | flops 86440016 | bytes 7116080 | solution.py:102
  184.8 5.4 collective-permute-done
  190.2 10.7 %conditional.3 = (bf16[16,4096]{1,0:T(8,128)(2,1)S(1)}, f32[128,512]{0,1:T(8,128)S(1)}, f32[128,512]{0,1:T(8,128)S(1)}, f32[4096]{0:T(1024)S(1)}, f32[4096]{0:T(1024)S(1)}) conditional(s32[]{:T(128)} %convert_element_type.83, () %tuple.67, (pred[]{:T(512)}, bf16[128,4096]{1,0:T(8,128)(2,1)}, s32[]{:T(128)}, bf16[16,4096]{1,0:T(8,128)(2,1)S(1)}, ...), branch_computations={%region_1.1_spmd, %region_2.9_spmd} | conditional | flops 86440016 | bytes 7116080 | solution.py:102
  202.4 5.4 collective-permute-done
  207.8 10.7 %conditional.3 = (bf16[16,4096]{1,0:T(8,128)(2,1)S(1)}, f32[128,512]{0,1:T(8,128)S(1)}, f32[128,512]{0,1:T(8,128)S(1)}, f32[4096]{0:T(1024)S(1)}, f32[4096]{0:T(1024)S(1)}) conditional(s32[]{:T(128)} %convert_element_type.83, () %tuple.67, (pred[]{:T(512)}, bf16[128,4096]{1,0:T(8,128)(2,1)}, s32[]{:T(128)}, bf16[16,4096]{1,0:T(8,128)(2,1)S(1)}, ...), branch_computations={%region_1.1_spmd, %region_2.9_spmd} | conditional | flops 86440016 | bytes 7116080 | solution.py:102
  220.0 5.4 collective-permute-done
  225.4 10.7 %conditional.3 = (bf16[16,4096]{1,0:T(8,128)(2,1)S(1)}, f32[128,512]{0,1:T(8,128)S(1)}, f32[128,512]{0,1:T(8,128)S(1)}, f32[4096]{0:T(1024)S(1)}, f32[4096]{0:T(1024)S(1)}) conditional(s32[]{:T(128)} %convert_element_type.83, () %tuple.67, (pred[]{:T(512)}, bf16[128,4096]{1,0:T(8,128)(2,1)}, s32[]{:T(128)}, bf16[16,4096]{1,0:T(8,128)(2,1)S(1)}, ...), branch_computations={%region_1.1_spmd, %region_2.9_spmd} | conditional | flops 86440016 | bytes 7116080 | solution.py:102
  237.6 5.4 collective-permute-done
  243.0 10.7 %conditional.3 = (bf16[16,4096]{1,0:T(8,128)(2,1)S(1)}, f32[128,512]{0,1:T(8,128)S(1)}, f32[128,512]{0,1:T(8,128)S(1)}, f32[4096]{0:T(1024)S(1)}, f32[4096]{0:T(1024)S(1)}) conditional(s32[]{:T(128)} %convert_element_type.83, () %tuple.67, (pred[]{:T(512)}, bf16[128,4096]{1,0:T(8,128)(2,1)}, s32[]{:T(128)}, bf16[16,4096]{1,0:T(8,128)(2,1)S(1)}, ...), branch_computations={%region_1.1_spmd, %region_2.9_spmd} | conditional | flops 86440016 | bytes 7116080 | solution.py:102
  255.2 4.2 collective-permute-done
  259.4 1.9 copy.59
  261.4 2.0 copy.57
  265.1 155.2 %reduce-scatter.9.cloned.1.call-done = f32[64,1]{1,0:T(8,128)} async-done(((f32[4096,1]{1,0:T(8,128)}), f32[64,1]{1,0:T(8,128)}) %reduce-scatter.9.cloned.1.call-update) | async-done | bytes 272
  420.3 1.3 copy.60
  421.7 151.4 %reduce-scatter.7.cloned.1.call-done = f32[64,1]{1,0:T(8,128)} async-done(((f32[4096,1]{1,0:T(8,128)}), f32[64,1]{1,0:T(8,128)}) %reduce-scatter.7.cloned.1.call-update) | async-done | bytes 272
  573.1 1.3 copy.58
  (306 shorter events, 106.7 us)
Async XLA Ops:
  7.2 413.1 %reduce-scatter.9.cloned.1.call-start = ((), (), s32[]{:S(2)}) async-start(), calls=%async_computation.3 | async-start | bytes 2129920
  7.5 6.4 %collective-permute-start = (bf16[16,4096]{1,0:T(8,128)(2,1)S(1)}, bf16[16,4096]{1,0:T(8,128)(2,1)S(1)}, u32[]{:S(2)}, u32[]{:S(2)}) collective-permute-start(bf16[16,4096]{1,0:T(8,128)(2,1)S(1)} %get-tuple-element.627), channel_id=1, source_target_pairs={{1,0},{2,1},{3,2},{4,3},{5,4},{6,5},{7,6},{9,8},{10,9},{11,10},{12... | collective-permute-start | bytes 393224 | tf_op jit(solution)/shard_map/while/body/eval_jaxpr/ppermute | solution.py:15
  14.0 7.6 %collective-permute-start = (bf16[16,4096]{1,0:T(8,128)(2,1)S(1)}, bf16[16,4096]{1,0:T(8,128)(2,1)S(1)}, u32[]{:S(2)}, u32[]{:S(2)}) collective-permute-start(bf16[16,4096]{1,0:T(8,128)(2,1)S(1)} %get-tuple-element.627), channel_id=1, source_target_pairs={{1,0},{2,1},{3,2},{4,3},{5,4},{6,5},{7,6},{9,8},{10,9},{11,10},{12... | collective-permute-start | bytes 393224 | tf_op jit(solution)/shard_map/while/body/eval_jaxpr/ppermute | solution.py:15
  21.7 6.2 %collective-permute-start = (bf16[16,4096]{1,0:T(8,128)(2,1)S(1)}, bf16[16,4096]{1,0:T(8,128)(2,1)S(1)}, u32[]{:S(2)}, u32[]{:S(2)}) collective-permute-start(bf16[16,4096]{1,0:T(8,128)(2,1)S(1)} %get-tuple-element.627), channel_id=1, source_target_pairs={{1,0},{2,1},{3,2},{4,3},{5,4},{6,5},{7,6},{9,8},{10,9},{11,10},{12... | collective-permute-start | bytes 393224 | tf_op jit(solution)/shard_map/while/body/eval_jaxpr/ppermute | solution.py:15
  28.0 5.7 collective-permute-start
  33.8 7.3 %collective-permute-start = (bf16[16,4096]{1,0:T(8,128)(2,1)S(1)}, bf16[16,4096]{1,0:T(8,128)(2,1)S(1)}, u32[]{:S(2)}, u32[]{:S(2)}) collective-permute-start(bf16[16,4096]{1,0:T(8,128)(2,1)S(1)} %get-tuple-element.627), channel_id=1, source_target_pairs={{1,0},{2,1},{3,2},{4,3},{5,4},{6,5},{7,6},{9,8},{10,9},{11,10},{12... | collective-permute-start | bytes 393224 | tf_op jit(solution)/shard_map/while/body/eval_jaxpr/ppermute | solution.py:15
  41.2 6.2 %collective-permute-start = (bf16[16,4096]{1,0:T(8,128)(2,1)S(1)}, bf16[16,4096]{1,0:T(8,128)(2,1)S(1)}, u32[]{:S(2)}, u32[]{:S(2)}) collective-permute-start(bf16[16,4096]{1,0:T(8,128)(2,1)S(1)} %get-tuple-element.627), channel_id=1, source_target_pairs={{1,0},{2,1},{3,2},{4,3},{5,4},{6,5},{7,6},{9,8},{10,9},{11,10},{12... | collective-permute-start | bytes 393224 | tf_op jit(solution)/shard_map/while/body/eval_jaxpr/ppermute | solution.py:15
  47.4 72.1 %collective-permute-start = (bf16[16,4096]{1,0:T(8,128)(2,1)S(1)}, bf16[16,4096]{1,0:T(8,128)(2,1)S(1)}, u32[]{:S(2)}, u32[]{:S(2)}) collective-permute-start(bf16[16,4096]{1,0:T(8,128)(2,1)S(1)} %get-tuple-element.627), channel_id=1, source_target_pairs={{1,0},{2,1},{3,2},{4,3},{5,4},{6,5},{7,6},{9,8},{10,9},{11,10},{12... | collective-permute-start | bytes 393224 | tf_op jit(solution)/shard_map/while/body/eval_jaxpr/ppermute | solution.py:15
  126.8 0.8 copy-start
  130.1 7.4 %collective-permute-start = (bf16[16,4096]{1,0:T(8,128)(2,1)S(1)}, bf16[16,4096]{1,0:T(8,128)(2,1)S(1)}, u32[]{:S(2)}, u32[]{:S(2)}) collective-permute-start(bf16[16,4096]{1,0:T(8,128)(2,1)S(1)} %get-tuple-element.627), channel_id=1, source_target_pairs={{1,0},{2,1},{3,2},{4,3},{5,4},{6,5},{7,6},{9,8},{10,9},{11,10},{12... | collective-permute-start | bytes 393224 | tf_op jit(solution)/shard_map/while/body/eval_jaxpr/ppermute | solution.py:15
  144.8 0.8 copy-start
  148.1 6.9 %collective-permute-start = (bf16[16,4096]{1,0:T(8,128)(2,1)S(1)}, bf16[16,4096]{1,0:T(8,128)(2,1)S(1)}, u32[]{:S(2)}, u32[]{:S(2)}) collective-permute-start(bf16[16,4096]{1,0:T(8,128)(2,1)S(1)} %get-tuple-element.627), channel_id=1, source_target_pairs={{1,0},{2,1},{3,2},{4,3},{5,4},{6,5},{7,6},{9,8},{10,9},{11,10},{12... | collective-permute-start | bytes 393224 | tf_op jit(solution)/shard_map/while/body/eval_jaxpr/ppermute | solution.py:15
  162.4 0.8 copy-start
  165.7 6.9 %collective-permute-start = (bf16[16,4096]{1,0:T(8,128)(2,1)S(1)}, bf16[16,4096]{1,0:T(8,128)(2,1)S(1)}, u32[]{:S(2)}, u32[]{:S(2)}) collective-permute-start(bf16[16,4096]{1,0:T(8,128)(2,1)S(1)} %get-tuple-element.627), channel_id=1, source_target_pairs={{1,0},{2,1},{3,2},{4,3},{5,4},{6,5},{7,6},{9,8},{10,9},{11,10},{12... | collective-permute-start | bytes 393224 | tf_op jit(solution)/shard_map/while/body/eval_jaxpr/ppermute | solution.py:15
  180.0 0.8 copy-start
  183.3 6.9 %collective-permute-start = (bf16[16,4096]{1,0:T(8,128)(2,1)S(1)}, bf16[16,4096]{1,0:T(8,128)(2,1)S(1)}, u32[]{:S(2)}, u32[]{:S(2)}) collective-permute-start(bf16[16,4096]{1,0:T(8,128)(2,1)S(1)} %get-tuple-element.627), channel_id=1, source_target_pairs={{1,0},{2,1},{3,2},{4,3},{5,4},{6,5},{7,6},{9,8},{10,9},{11,10},{12... | collective-permute-start | bytes 393224 | tf_op jit(solution)/shard_map/while/body/eval_jaxpr/ppermute | solution.py:15
  197.6 0.8 copy-start
  200.9 6.9 %collective-permute-start = (bf16[16,4096]{1,0:T(8,128)(2,1)S(1)}, bf16[16,4096]{1,0:T(8,128)(2,1)S(1)}, u32[]{:S(2)}, u32[]{:S(2)}) collective-permute-start(bf16[16,4096]{1,0:T(8,128)(2,1)S(1)} %get-tuple-element.627), channel_id=1, source_target_pairs={{1,0},{2,1},{3,2},{4,3},{5,4},{6,5},{7,6},{9,8},{10,9},{11,10},{12... | collective-permute-start | bytes 393224 | tf_op jit(solution)/shard_map/while/body/eval_jaxpr/ppermute | solution.py:15
  215.1 0.8 copy-start
  218.5 6.9 %collective-permute-start = (bf16[16,4096]{1,0:T(8,128)(2,1)S(1)}, bf16[16,4096]{1,0:T(8,128)(2,1)S(1)}, u32[]{:S(2)}, u32[]{:S(2)}) collective-permute-start(bf16[16,4096]{1,0:T(8,128)(2,1)S(1)} %get-tuple-element.627), channel_id=1, source_target_pairs={{1,0},{2,1},{3,2},{4,3},{5,4},{6,5},{7,6},{9,8},{10,9},{11,10},{12... | collective-permute-start | bytes 393224 | tf_op jit(solution)/shard_map/while/body/eval_jaxpr/ppermute | solution.py:15
  232.7 0.8 copy-start
  236.0 6.9 %collective-permute-start = (bf16[16,4096]{1,0:T(8,128)(2,1)S(1)}, bf16[16,4096]{1,0:T(8,128)(2,1)S(1)}, u32[]{:S(2)}, u32[]{:S(2)}) collective-permute-start(bf16[16,4096]{1,0:T(8,128)(2,1)S(1)} %get-tuple-element.627), channel_id=1, source_target_pairs={{1,0},{2,1},{3,2},{4,3},{5,4},{6,5},{7,6},{9,8},{10,9},{11,10},{12... | collective-permute-start | bytes 393224 | tf_op jit(solution)/shard_map/while/body/eval_jaxpr/ppermute | solution.py:15
  250.3 0.8 copy-start
  253.6 5.7 collective-permute-start
  259.4 2.0 copy-start.1
  261.3 311.7 %reduce-scatter.7.cloned.1.call-start = ((), (), s32[]{:S(2)}) async-start(), calls=%async_computation.2 | async-start | bytes 2129920
Sparse Core Ops, SparseCore 0:
  261.4 158.8 reduce-scatter.8
  425.6 147.3 reduce-scatter.6
where the time goes:
time: 587 us; the launch traced here: 581 us
  waiting for transfers between devices  450 us (77%)
  other arithmetic  60.6 us (10%)
  local copies, waits for them, and re-layouts  24.9 us (4%)
  starting transfers between devices  19.5 us (3%)
  between operations  14.1 us (2%)
  matrix products  10.3 us (2%)
    unnamed x4, waiting for transfers between devices  307 us
    ppermute x15, waiting for transfers between devices, shifted(): return lax.ppermute(array, axis, pairs)  143 us
    ppermute x15, starting transfers between devices, shifted(): return lax.ppermute(array, axis, pairs)  19.4 us
    cond x16, other arithmetic  16.7 us
  transfers between devices with their start and end apart: 17, of which 17 were waited for; matrix products, arithmetic and copies ran while one was open for 1% of the time, Pallas kernels for 0%

commit v1 on v0

v1 whole, which is shorter than its diff:
```python
import functools

import jax
import jax.numpy as jnp
from jax import lax
from jax.experimental import pallas as pl
from jax.experimental.pallas import tpu as pltpu
from jax.sharding import PartitionSpec as P

MESH = pl.DeviceIdType.MESH
HD = 128
KVH = 4
SEQ = 128
WIDTH = 4096
ROWS = 4
SPANS = SEQ // ROWS
BLOCK = 16
BLOCKS = SEQ // BLOCK
PER_BLOCK = BLOCK // ROWS
HALF = 16
DP_X, DP_Z, DP_CORE = 4, 8, 2
FACTOR = HD ** (-0.5)
F32, BF16 = jnp.float32, jnp.bfloat16


def dot(a, b):
    return jnp.dot(a, b, preferred_element_type=F32)


def low_of(rows):
    return (lax.broadcasted_iota(jnp.int32, (rows, HD), 0) & 7) < 4


def pick(wide, low):
    return jnp.where(low, wide[:, :HD], wide[:, HD:])


def spread(narrow, low):
    zero = jnp.zeros_like(narrow)
    return jnp.concatenate([jnp.where(low, narrow, zero), jnp.where(low, zero, narrow)], axis=1)


def tiled(eight, times):
    return jnp.concatenate([eight] * times, axis=0)


def pack(eight_rows, low8):
    first, second = [], []
    for h in range(HALF):
        a = eight_rows[:, h * HD : (h + 1) * HD]
        b = eight_rows[:, (h + HALF) * HD : (h + HALF + 1) * HD]
        first.append(jnp.where(low8, a, pltpu.roll(b, 4, 0)))
        second.append(jnp.where(low8, pltpu.roll(a, 4, 0), b))
    return jnp.concatenate(first, axis=0), jnp.concatenate(second, axis=0)


def kernel(
    sections,
    x_hbm, k_hbm, v_hbm, top_hbm, gain_hbm, bias_hbm, length_ref,
    out_ref, key_out, value_out, gain_out, bias_out,
    x_v, top_v, k_v, v_v, gain_v, bias_v,
    keys, values, keys_t, values_t, gain_p, bias_p,
    arrived, sent, norm_p, inv_p, probs_p, mix_p, base_p,
    query_b, probs_b, grads_b, gain_acc, bias_acc,
    first_src, first_dst, second_src, second_dst,
    in_sem, x_sem, top_sem, send_sem, recv_sem, s1_send, s1_recv, s2_send, s2_recv,
):
    section = lax.axis_index("section")
    me = lax.axis_index("dp")
    px, pz, pc = me // 16, (me // 2) % 8, me % 2
    above, below = (section + 1) % sections, (section + sections - 1) % sections
    is_top = section == sections - 1

    def x_copy(b):
        rows = pl.ds(b * BLOCK, BLOCK)
        return pltpu.make_async_copy(x_hbm.at[rows], x_v.at[rows], x_sem.at[b])

    def top_copy(b):
        rows = pl.ds(b * BLOCK, BLOCK)
        return pltpu.make_async_copy(top_hbm.at[rows], top_v.at[rows], top_sem.at[b])

    small = [
        pltpu.make_async_copy(src, dst, in_sem.at[i])
        for i, (src, dst) in enumerate(
            [(k_hbm, k_v), (v_hbm, v_v), (gain_hbm, gain_v), (bias_hbm, bias_v)]
        )
    ]
    for copy in small:
        copy.start()
    for b in range(BLOCKS):
        x_copy(b).start()

    @pl.when(is_top)
    def _():
        for b in range(BLOCKS):
            top_copy(b).start()

    def first_peer(k):
        return {"dp": px * 16 + ((pz + k // 2) % 8) * 2 + (pc + k % 2) % 2}

    def second_peer(k):
        return {"dp": ((px + k) % 4) * 16 + pz * 2 + pc}

    barrier = pltpu.get_barrier_semaphore()
    peers = [{"section": above}, {"section": below}]
    peers += [first_peer(k) for k in range(1, 16)] + [second_peer(k) for k in range(1, 4)]
    for peer in peers:
        pl.semaphore_signal(barrier, inc=1, device_id=peer, device_id_type=MESH)

    low8, low64, low128 = low_of(8), low_of(64), low_of(128)
    for copy in small:
        copy.wait()
    for p in range(2):
        for src, dst, dst_t in ((k_v, keys, keys_t), (v_v, values, values_t)):
            for j in range(2):
                part = src[:, (p + 2 * j) * HD : (p + 2 * j + 1) * HD]
                dst[p, j * SEQ : (j + 1) * SEQ, :] = part
                dst_t[p, :, j * SEQ : (j + 1) * SEQ] = part.T
    for src, dst in ((gain_v, gain_p), (bias_v, bias_p)):
        for h in range(HALF):
            a = jnp.broadcast_to(src[:, h * HD : (h + 1) * HD], (8, HD))
            b = jnp.broadcast_to(src[:, (h + HALF) * HD : (h + HALF + 1) * HD], (8, HD))
            dst[h * 8 : (h + 1) * 8, :] = jnp.where(low8, a, b)
    gain_acc[...] = jnp.zeros_like(gain_acc)
    bias_acc[...] = jnp.zeros_like(bias_acc)
    length = length_ref[0]
    columns = lax.broadcasted_iota(jnp.int32, (8, HD), 1)
    offsets = lax.broadcasted_iota(jnp.int32, (8, HD), 0) & 3

    pl.semaphore_wait(barrier, len(peers))

    def forward(b):
        x_copy(b).wait()
        inputs = x_v[pl.ds(b * BLOCK, BLOCK), :].astype(F32)
        inverse = lax.rsqrt(jnp.mean(inputs * inputs, -1, keepdims=True) + 1e-06)
        normed = inputs * inverse
        inverse = jnp.broadcast_to(inverse, (BLOCK, HD))
        gains, biases = gain_p[...], bias_p[...]
        for half in range(2):
            rows = slice(half * 8, half * 8 + 8)
            pair = pack(normed[rows], low8)
            inv = inverse[rows]
            flipped = pltpu.roll(inv, 4, 0)
            pair_inv = (jnp.where(low8, inv, flipped), jnp.where(low8, flipped, inv))
            for j in range(2):
                span = b * PER_BLOCK + half * 2 + j
                norm = pair[j]
                norm_p[span] = norm
                inv_p[span] = pair_inv[j]
                gained = norm * gains
                query = (gained + biases).astype(BF16)
                gained = gained.astype(BF16)
                position = span * ROWS + offsets
                live = tiled(jnp.where(position < length, 1.0, 0.0).astype(F32), 8)
                allowed = tiled(
                    jnp.where((columns <= position) & (columns < length), 1.0, 0.0).astype(F32), 8
                )
                for p in range(2):
                    part = slice(64 * p, 64 * p + 64)
                    query_b[p, span] = query[part]
                    both = dot(jnp.concatenate([query[part], gained[part]], axis=0), keys_t[p])
                    both = pick(both, low128)
                    scores = jnp.where(allowed > 0.5, both[:64] * FACTOR, -1e30)
                    mix_p[span, part, :] = both[64:]
                    weights = jnp.exp(scores - jnp.max(scores, -1, keepdims=True))
                    weights = weights * (1.0 / jnp.sum(weights, -1, keepdims=True)) * live
                    probs_p[span, part, :] = weights * FACTOR
                    wide = spread(weights, low64)
                    high = wide.astype(BF16)
                    probs_b[p, span] = high
                    rest = (wide - high.astype(F32)).astype(BF16)
                    outs = dot(jnp.concatenate([high, rest], axis=0), values[p])
                    base_p[span, part, :] = outs[:64] + outs[64:]

    def take_top(b):
        top_copy(b).wait()
        rows = top_v[pl.ds(b * BLOCK, BLOCK), :].astype(F32)
        for half in range(2):
            pair = pack(rows[half * 8 : half * 8 + 8], low8)
            for j in range(2):
                arrived[b * PER_BLOCK + half * 2 + j] = pair[j].astype(BF16)

    def hop(i):
        return pltpu.make_async_remote_copy(
            src_ref=sent.at[i],
            dst_ref=arrived.at[i],
            send_sem=send_sem.at[i],
            recv_sem=recv_sem.at[i],
            device_id={"section": below},
            device_id_type=MESH,
        )

    def backward(i):
        @pl.when(jnp.logical_not(is_top))
        def _():
            hop(i).wait_recv()

        upstream = arrived[i]
        wide = upstream.astype(F32)
        centre = jnp.sum(wide * base_p[i], -1, keepdims=True)
        queries, kept, totals = [], [], jnp.zeros((8, HD), F32)
        for p in range(2):
            part = slice(64 * p, 64 * p + 64)
            grad_probs = pick(dot(upstream[part], values_t[p]), low64)
            grads = probs_p[i, part, :] * (grad_probs - centre[part])
            totals = totals + jnp.sum((grads * mix_p[i, part, :]).reshape(8, 8, HD), axis=0)
            grads_wide = spread(grads, low64).astype(BF16)
            kept.append(grads_wide)
            queries.append(dot(grads_wide, keys[p]))
        mean = jnp.sum(totals, -1, keepdims=True) * (1.0 / WIDTH)
        mean = jnp.broadcast_to(mean, (8, HD))
        mean = mean + pltpu.roll(mean, 4, 0)
        grad_query = jnp.concatenate(queries, axis=0)
        norm = norm_p[i]
        change = grad_query * gain_p[...] - norm * tiled(mean, HALF)
        sent[i] = (wide + tiled(inv_p[i], HALF) * change).astype(BF16)

        @pl.when(section > 0)
        def _():
            hop(i).start()

        for p in range(2):
            grads_b[p, i] = kept[p]
        gain_acc[...] += grad_query * norm
        bias_acc[...] += grad_query

    lead = jnp.where(is_top, 0, jnp.where(section == sections - 2, 2, BLOCKS - 1))

    def turn(t, carry):
        @pl.when(t < BLOCKS)
        def _():
            @pl.when(is_top)
            def _():
                take_top(t)

            forward(t)

        @pl.when(t >= lead)
        def _():
            def step(q, c):
                backward((t - lead) * PER_BLOCK + q)
                return c

            lax.fori_loop(0, PER_BLOCK, step, 0)

        return carry

    lax.fori_loop(0, BLOCKS + lead, turn, 0)

    for g, acc in enumerate((gain_acc, bias_acc)):
        terms = acc[...].reshape(HALF, 8, HD)
        halves = (jnp.sum(terms[:, :4], axis=1), jnp.sum(terms[:, 4:], axis=1))
        for x in range(DP_X):
            rows = halves[x // 2][(x % 2) * 8 : (x % 2) * 8 + 8]
            for z in range(DP_Z):
                first_src[z, 2 * x + g : 2 * x + g + 1, :] = rows[z : z + 1]

    def first_copy(k):
        return pltpu.make_async_remote_copy(
            src_ref=first_src.at[(pz + k // 2) % 8],
            dst_ref=first_dst.at[k],
            send_sem=s1_send.at[k],
            recv_sem=s1_recv.at[k],
            device_id=first_peer(k),
            device_id_type=MESH,
        )

    def second_copy(k):
        return pltpu.make_async_remote_copy(
            src_ref=second_src.at[(px + k) % 4],
            dst_ref=second_dst.at[k],
            send_sem=s2_send.at[k],
            recv_sem=s2_recv.at[k],
            device_id=second_peer(k),
            device_id_type=MESH,
        )

    for k in range(1, 16):
        first_copy(k).start()

    flat = SPANS * 64

    def contract(left, right):
        return lax.dot_general(left, right, (((0,), (0,)), ((), ())), preferred_element_type=F32)

    for p in range(2):
        got = arrived[:, 64 * p : 64 * p + 64, :].reshape(flat, HD)
        value_grad = contract(probs_b[p].reshape(flat, 2 * SEQ), got)
        for j in range(2):
            head = p + 2 * j
            value_out[:, head * HD : (head + 1) * HD] = value_grad[j * SEQ : (j + 1) * SEQ]

    total = first_src[pz]
    for k in range(1, 16):
        first_copy(k).wait_recv()
        total = total + first_dst[k]
    for x in range(DP_X):
        second_src[x] = total[2 * x : 2 * x + 2]
    for k in range(1, 4):
        second_copy(k).start()

    for p in range(2):
        key_grad = contract(grads_b[p].reshape(flat, 2 * SEQ), query_b[p].reshape(flat, HD))
        for j in range(2):
            head = p + 2 * j
            key_out[:, head * HD : (head + 1) * HD] = key_grad[j * SEQ : (j + 1) * SEQ]

    def unpack(b, carry):
        parts = [sent[b * PER_BLOCK + j].astype(F32) for j in range(PER_BLOCK)]
        for h in range(HALF):
            tiles = [part[h * 8 : h * 8 + 8] for part in parts]
            turned = [pltpu.roll(tile, 4, 0) for tile in tiles]
            lower = [jnp.where(low8, tiles[j], turned[j + 1]) for j in (0, 2)]
            upper = [jnp.where(low8, turned[j], tiles[j + 1]) for j in (0, 2)]
            for head, pieces in ((h, lower), (h + HALF, upper)):
                out_ref[pl.ds(b * BLOCK, BLOCK), head * HD : (head + 1) * HD] = jnp.concatenate(
                    pieces, axis=0
                ).astype(BF16)
        return carry

    lax.fori_loop(0, BLOCKS, unpack, 0)

    share = second_src[px]
    for k in range(1, 4):
        second_copy(k).wait_recv()
        share = share + second_dst[k]
    share = jnp.where(pc == 0, share, pltpu.roll(share, HD // 2, 1))
    gain_out[...] = share[0:1, : HD // 2]
    bias_out[...] = share[1:2, : HD // 2]

    def sent_all(i, carry):
        hop(i).wait_send()
        return carry

    @pl.when(section > 0)
    def _():
        lax.fori_loop(0, SPANS, sent_all, 0)

    for k in range(1, 16):
        first_copy(k).wait_send()
    for k in range(1, 4):
        second_copy(k).wait_send()


def local(sections, layer_input, keys, values, top_grad, gains, biases, lengths):
    anywhere = pl.BlockSpec(memory_space=pl.ANY)
    vmem = pl.BlockSpec(memory_space=pltpu.VMEM)
    kv = KVH * HD
    dma = pltpu.SemaphoreType.DMA
    span = (SPANS, 128, HD)
    outs = pl.pallas_call(
        functools.partial(kernel, sections),
        out_shape=(
            jax.ShapeDtypeStruct((SEQ, WIDTH), BF16),
            jax.ShapeDtypeStruct((SEQ, kv), F32),
            jax.ShapeDtypeStruct((SEQ, kv), F32),
            jax.ShapeDtypeStruct((1, HD // 2), F32),
            jax.ShapeDtypeStruct((1, HD // 2), F32),
        ),
        in_specs=[anywhere] * 6 + [pl.BlockSpec(memory_space=pltpu.SMEM)],
        out_specs=(vmem,) * 5,
        scratch_shapes=[
            pltpu.VMEM((SEQ, WIDTH), BF16),
            pltpu.VMEM((SEQ, WIDTH), BF16),
            pltpu.VMEM((SEQ, kv), BF16),
            pltpu.VMEM((SEQ, kv), BF16),
            pltpu.VMEM((1, WIDTH), F32),
            pltpu.VMEM((1, WIDTH), F32),
            pltpu.VMEM((2, 2 * SEQ, HD), BF16),
            pltpu.VMEM((2, 2 * SEQ, HD), BF16),
            pltpu.VMEM((2, HD, 2 * SEQ), BF16),
            pltpu.VMEM((2, HD, 2 * SEQ), BF16),
            pltpu.VMEM((128, HD), F32),
            pltpu.VMEM((128, HD), F32),
            pltpu.VMEM(span, BF16),
            pltpu.VMEM(span, BF16),
            pltpu.VMEM(span, F32),
            pltpu.VMEM((SPANS, 8, HD), F32),
            pltpu.VMEM(span, F32),
            pltpu.VMEM(span, F32),
            pltpu.VMEM(span, F32),
            pltpu.VMEM((2, SPANS, 64, HD), BF16),
            pltpu.VMEM((2, SPANS, 64, 2 * SEQ), BF16),
            pltpu.VMEM((2, SPANS, 64, 2 * SEQ), BF16),
            pltpu.VMEM((128, HD), F32),
            pltpu.VMEM((128, HD), F32),
            pltpu.VMEM((DP_Z, 8, HD), F32),
            pltpu.VMEM((16, 8, HD), F32),
            pltpu.VMEM((DP_X, 2, HD), F32),
            pltpu.VMEM((DP_X, 2, HD), F32),
            dma((4,)),
            dma((BLOCKS,)),
            dma((BLOCKS,)),
            dma((SPANS,)),
            dma((SPANS,)),
            dma((16,)),
            dma((16,)),
            dma((4,)),
            dma((4,)),
        ],
        compiler_params=pltpu.CompilerParams(
            collective_id=0, has_side_effects=True, vmem_limit_bytes=48 << 20
        ),
    )(layer_input[0, 0], keys[0, 0], values[0, 0], top_grad[0], gains, biases, lengths)
    grad_in, key_grad, value_grad, gain_grad, bias_grad = outs
    return grad_in[None, None], key_grad[None, None], value_grad[None, None], gain_grad, bias_grad


def solution(mesh):
    return jax.shard_map(
        functools.partial(local, mesh.shape["section"]),
        mesh=mesh,
        in_specs=(
            P("section", "dp", None, None),
            P("section", "dp", None, None),
            P("section", "dp", None, None),
            P("dp", None, None),
            P("section", None),
            P("section", None),
            P("dp"),
        ),
        out_specs=(
            P("section", "dp", None, None),
            P("section", "dp", None, None),
            P("section", "dp", None, None),
            P("section", "dp"),
            P("section", "dp"),
        ),
        check_vma=False,
    )
```

time: 587 us -> 83.1 us (0.14)
  waiting for transfers between devices: 450 us -> 0 us
  Pallas kernels: 0 us -> 72.3 us
  other arithmetic: 60.6 us -> 0 us
  starting transfers between devices: 19.5 us -> 0 us
  local copies, waits for them, and re-layouts: 24.9 us -> 9.08 us
  between operations: 14.1 us -> 1.3 us
  matrix products: 10.3 us -> 0 us
    unnamed x4 -> x0, waiting for transfers between devices: 307 us -> none
    ppermute x15 -> x0, waiting for transfers between devices: 143 us -> none  [shifted(): return lax.ppermute(array, axis, pairs)]
    pallas_call x0 -> x1, Pallas kernels: none -> 72.3 us  [local(): pl.pallas_call(functools.partial(kernel, sections), out_shape=(jax.ShapeD...]
    ppermute x15 -> x0, starting transfers between devices: 19.4 us -> none  [shifted(): return lax.ppermute(array, axis, pairs)]
    reduce_sum x16 -> x0, other arithmetic: 18.7 us -> none  [the longest x8 10 us: block_grad(): gain_part = jnp.sum(grad_query * normed, 0)]
    cond x16 -> x0, other arithmetic: 16.7 us -> none
    another operation x52 -> x0, local copies, waits for them, and re-layouts: 15.5 us -> none  [the longest x8 7.53 us: block_grad(): key_heads = key_rows.reshape(seqlen, KVH, HD)]
    convert_element_type x16 -> x0, other arithmetic: 15.3 us -> none  [the longest x8 10.1 us: block_grad(): result = (upstream.astype(jnp.float32) + grad_inputs).astype(jnp.bfloat16)]
  transfers between devices with their start and end apart: 17 -> 0, of which waited for: 17 -> 0; matrix products, arithmetic and copies ran while one was open for 1% -> 0% of each run, Pallas kernels for 0% -> 0%
where the time goes in v1:
time: 83.1 us; the launch traced here: 82.7 us
  Pallas kernels  72.3 us (87%)
  local copies, waits for them, and re-layouts  9.08 us (11%)
  between operations  1.3 us (2%)
    pallas_call x1, Pallas kernels, local(): pl.pallas_call(functools.partial(kernel, sections), out_shape=(jax.ShapeD...  72.3 us
    unnamed x17, local copies, waits for them, and re-layouts  9.08 us

profile of v1, /device:TPU:1, one launch (start us, length us, event | category | flops | bytes accessed | tf_op | source)
XLA Modules:
  0.0 82.7 jit_solution(8915703641100719884)
XLA Ops:
  1.3 0.0 copy-start
  1.3 1.2 %copy-done = bf16[1,1,128,4096]{3,2,1,0:T(8,128)(2,1)S(1)} copy-done((bf16[1,1,128,4096]{3,2,1,0:T(8,128)(2,1)S(1)}, bf16[1,1,128,4096]{3,2,1,0:T(8,128)(2,1)}, u32[]{:S(2)}) %copy-start) | copy-done | bytes 1048600
  2.5 0.0 copy-start.1
  2.5 1.2 %copy-done.1 = bf16[1,128,4096]{2,1,0:T(8,128)(2,1)S(1)} copy-done((bf16[1,128,4096]{2,1,0:T(8,128)(2,1)S(1)}, bf16[1,128,4096]{2,1,0:T(8,128)(2,1)}, u32[]{:S(2)}) %copy-start.1) | copy-done | bytes 1048600
  3.7 0.0 copy-start.2
  3.7 0.9 %copy-done.2 = bf16[1,1,128,512]{3,2,1,0:T(8,128)(2,1)S(1)} copy-done((bf16[1,1,128,512]{3,2,1,0:T(8,128)(2,1)S(1)}, bf16[1,1,128,512]{3,2,1,0:T(8,128)(2,1)}, u32[]{:S(2)}) %copy-start.2) | copy-done | bytes 131096
  4.6 0.0 copy-start.3
  4.6 0.9 %copy-done.3 = bf16[1,1,128,512]{3,2,1,0:T(8,128)(2,1)S(1)} copy-done((bf16[1,1,128,512]{3,2,1,0:T(8,128)(2,1)S(1)}, bf16[1,1,128,512]{3,2,1,0:T(8,128)(2,1)}, u32[]{:S(2)}) %copy-start.3) | copy-done | bytes 131096
  5.5 0.0 copy-start.4
  5.5 0.7 copy-done.4
  6.3 0.0 copy-start.5
  6.3 0.7 copy-done.5
  7.0 72.3 %shard_map.110 = (bf16[128,4096]{1,0:T(8,128)(2,1)S(1)}, f32[128,512]{1,0:T(8,128)S(1)}, f32[128,512]{1,0:T(8,128)S(1)}, f32[1,64]{1,0:T(1,128)S(1)}, f32[1,64]{1,0:T(1,128)S(1)}) custom-call(bf16[128,4096]{1,0:T(8,128)(2,1)S(1)} %bitcast.8, bf16[128,512]{1,0:T(8,128)(2,1)S(1)} %bitcast.12, bf16[128,512]{1,0:T(8,128)(2,1)S(1)} %bitcast.13, ...), custom_call_target="tpu_custom_call" | custom-call | tf_op jit(solution)/shard_map/pallas_call | solution.py:351
  79.3 1.0 %copy.18 = bf16[1,1,128,4096]{3,2,1,0:T(8,128)(2,1)} copy(bf16[1,1,128,4096]{3,2,1,0:T(8,128)(2,1)S(1)} %bitcast.7) | data formatting | bytes 2097152
  80.3 0.7 copy.19
  81.0 0.7 copy.20
  81.7 0.5 copy.21
  82.2 0.5 copy.22
Async XLA Ops:
  1.3 1.2 %copy-start = (bf16[1,1,128,4096]{3,2,1,0:T(8,128)(2,1)S(1)}, bf16[1,1,128,4096]{3,2,1,0:T(8,128)(2,1)}, u32[]{:S(2)}) copy-start(bf16[1,1,128,4096]{3,2,1,0:T(8,128)(2,1)} %param.7) | copy-start | bytes 3145732
  2.5 1.2 %copy-start.1 = (bf16[1,128,4096]{2,1,0:T(8,128)(2,1)S(1)}, bf16[1,128,4096]{2,1,0:T(8,128)(2,1)}, u32[]{:S(2)}) copy-start(bf16[1,128,4096]{2,1,0:T(8,128)(2,1)} %param.10) | copy-start | bytes 3145732
  3.7 0.9 %copy-start.2 = (bf16[1,1,128,512]{3,2,1,0:T(8,128)(2,1)S(1)}, bf16[1,1,128,512]{3,2,1,0:T(8,128)(2,1)}, u32[]{:S(2)}) copy-start(bf16[1,1,128,512]{3,2,1,0:T(8,128)(2,1)} %param.8) | copy-start | bytes 393220
  4.6 0.9 %copy-start.3 = (bf16[1,1,128,512]{3,2,1,0:T(8,128)(2,1)S(1)}, bf16[1,1,128,512]{3,2,1,0:T(8,128)(2,1)}, u32[]{:S(2)}) copy-start(bf16[1,1,128,512]{3,2,1,0:T(8,128)(2,1)} %param.9) | copy-start | bytes 393220
  5.5 0.7 copy-start.4
  6.3 0.7 copy-start.5

commit v2 on v1

--- a/solution.py
+++ b/solution.py
@@ -70,6 +70,7 @@
     px, pz, pc = me // 16, (me // 2) % 8, me % 2
     above, below = (section + 1) % sections, (section + sections - 1) % sections
     is_top = section == sections - 1
+    held_back = is_top & (pc == 1)
 
     def x_copy(b):
         rows = pl.ds(b * BLOCK, BLOCK)
@@ -99,11 +100,11 @@
         return {"dp": px * 16 + ((pz + k // 2) % 8) * 2 + (pc + k % 2) % 2}
 
     def second_peer(k):
-        return {"dp": ((px + k) % 4) * 16 + pz * 2 + pc}
+        return {"dp": ((px + k // 2) % 4) * 16 + pz * 2 + (pc + k % 2) % 2}
 
     barrier = pltpu.get_barrier_semaphore()
     peers = [{"section": above}, {"section": below}]
-    peers += [first_peer(k) for k in range(1, 16)] + [second_peer(k) for k in range(1, 4)]
+    peers += [first_peer(k) for k in range(1, 16)] + [second_peer(k) for k in range(2, 8)]
     for peer in peers:
         pl.semaphore_signal(barrier, inc=1, device_id=peer, device_id_type=MESH)
 
@@ -126,8 +127,6 @@
     length = length_ref[0]
     columns = lax.broadcasted_iota(jnp.int32, (8, HD), 1)
     offsets = lax.broadcasted_iota(jnp.int32, (8, HD), 0) & 3
-
-    pl.semaphore_wait(barrier, len(peers))
 
     def forward(b):
         x_copy(b).wait()
@@ -215,26 +214,33 @@
         change = grad_query * gain_p[...] - norm * tiled(mean, HALF)
         sent[i] = (wide + tiled(inv_p[i], HALF) * change).astype(BF16)
 
-        @pl.when(section > 0)
+        @pl.when((section > 0) & jnp.logical_not(held_back))
         def _():
             hop(i).start()
+
+        @pl.when(held_back & (i % 2 == 1))
+        def _():
+            hop(i // 2).start()
 
         for p in range(2):
             grads_b[p, i] = kept[p]
         gain_acc[...] += grad_query * norm
         bias_acc[...] += grad_query
 
-    lead = jnp.where(is_top, 0, jnp.where(section == sections - 2, 2, BLOCKS - 1))
+    behind = sections - 1 - section
+    lead = jnp.where(behind == 0, 0, jnp.where(behind == 1, 3, jnp.where(behind == 2, 6, BLOCKS - 1)))
+
+    def prepare(b):
+        @pl.when(is_top)
+        def _():
+            take_top(b)
+
+        forward(b)
+
+    prepare(0)
+    pl.semaphore_wait(barrier, len(peers))
 
     def turn(t, carry):
-        @pl.when(t < BLOCKS)
-        def _():
-            @pl.when(is_top)
-            def _():
-                take_top(t)
-
-            forward(t)
-
         @pl.when(t >= lead)
         def _():
             def step(q, c):
@@ -243,9 +249,21 @@
 
             lax.fori_loop(0, PER_BLOCK, step, 0)
 
+        @pl.when(t + 1 < BLOCKS)
+        def _():
+            prepare(t + 1)
+
         return carry
 
     lax.fori_loop(0, BLOCKS + lead, turn, 0)
+
+    @pl.when(held_back)
+    def _():
+        def late(i, carry):
+            hop(i).start()
+            return carry
+
+        lax.fori_loop(SPANS // 2, SPANS, late, 0)
 
     for g, acc in enumerate((gain_acc, bias_acc)):
         terms = acc[...].reshape(HALF, 8, HD)
@@ -253,11 +271,11 @@
         for x in range(DP_X):
             rows = halves[x // 2][(x % 2) * 8 : (x % 2) * 8 + 8]
             for z in range(DP_Z):
-                first_src[z, 2 * x + g : 2 * x + g + 1, :] = rows[z : z + 1]
+                first_src[g, z, x : x + 1, :] = rows[z : z + 1]
 
     def first_copy(k):
         return pltpu.make_async_remote_copy(
-            src_ref=first_src.at[(pz + k // 2) % 8],
+            src_ref=first_src.at[(pc + k % 2) % 2, (pz + k // 2) % 8],
             dst_ref=first_dst.at[k],
             send_sem=s1_send.at[k],
             recv_sem=s1_recv.at[k],
@@ -267,7 +285,7 @@
 
     def second_copy(k):
         return pltpu.make_async_remote_copy(
-            src_ref=second_src.at[(px + k) % 4],
+            src_ref=second_src.at[(px + k // 2) % 4],
             dst_ref=second_dst.at[k],
             send_sem=s2_send.at[k],
             recv_sem=s2_recv.at[k],
@@ -290,13 +308,13 @@
             head = p + 2 * j
             value_out[:, head * HD : (head + 1) * HD] = value_grad[j * SEQ : (j + 1) * SEQ]
 
-    total = first_src[pz]
+    total = first_src[pc, pz]
     for k in range(1, 16):
         first_copy(k).wait_recv()
         total = total + first_dst[k]
     for x in range(DP_X):
-        second_src[x] = total[2 * x : 2 * x + 2]
-    for k in range(1, 4):
+        second_src[x] = total[x : x + 1]
+    for k in range(1, 8):
         second_copy(k).start()
 
     for p in range(2):
@@ -320,13 +338,14 @@
 
     lax.fori_loop(0, BLOCKS, unpack, 0)
 
-    share = second_src[px]
-    for k in range(1, 4):
+    shares = [second_src[px], jnp.zeros((1, HD), F32)]
+    for k in range(1, 8):
         second_copy(k).wait_recv()
-        share = share + second_dst[k]
-    share = jnp.where(pc == 0, share, pltpu.roll(share, HD // 2, 1))
-    gain_out[...] = share[0:1, : HD // 2]
-    bias_out[...] = share[1:2, : HD // 2]
+        shares[k % 2] = shares[k % 2] + second_dst[k]
+    gain = jnp.where(pc == 0, shares[0], pltpu.roll(shares[1], HD // 2, 1))
+    bias = jnp.where(pc == 0, shares[1], pltpu.roll(shares[0], HD // 2, 1))
+    gain_out[...] = gain[:, : HD // 2]
+    bias_out[...] = bias[:, : HD // 2]
 
     def sent_all(i, carry):
         hop(i).wait_send()
@@ -338,12 +357,23 @@
 
     for k in range(1, 16):
         first_copy(k).wait_send()
-    for k in range(1, 4):
+    for k in range(1, 8):
         second_copy(k).wait_send()
 
 
+def write(*refs):
+    count = len(refs) // 2
+    copies = [
+        pltpu.make_async_copy(refs[i], refs[count + i], refs[-1].at[i]) for i in range(count)
+    ]
+    for copy in copies:
+        copy.start()
+    for copy in copies:
+        copy.wait()
+
+
 def local(sections, layer_input, keys, values, top_grad, gains, biases, lengths):
-    anywhere = pl.BlockSpec(memory_space=pl.ANY)
+    anywhere = pl.BlockSpec(memory_space=pltpu.HBM)
     vmem = pl.BlockSpec(memory_space=pltpu.VMEM)
     kv = KVH * HD
     dma = pltpu.SemaphoreType.DMA
@@ -384,10 +414,10 @@
             pltpu.VMEM((2, SPANS, 64, 2 * SEQ), BF16),
             pltpu.VMEM((128, HD), F32),
             pltpu.VMEM((128, HD), F32),
-            pltpu.VMEM((DP_Z, 8, HD), F32),
-            pltpu.VMEM((16, 8, HD), F32),
-            pltpu.VMEM((DP_X, 2, HD), F32),
-            pltpu.VMEM((DP_X, 2, HD), F32),
+            pltpu.VMEM((DP_CORE, DP_Z, DP_X, HD), F32),
+            pltpu.VMEM((DP_Z * DP_CORE, DP_X, HD), F32),
+            pltpu.VMEM((DP_X, 1, HD), F32),
+            pltpu.VMEM((DP_X * DP_CORE, 1, HD), F32),
             dma((4,)),
             dma((BLOCKS,)),
             dma((BLOCKS,)),
@@ -395,14 +425,21 @@
             dma((SPANS,)),
             dma((16,)),
             dma((16,)),
-            dma((4,)),
-            dma((4,)),
+            dma((8,)),
+            dma((8,)),
         ],
         compiler_params=pltpu.CompilerParams(
-            collective_id=0, has_side_effects=True, vmem_limit_bytes=48 << 20
+            collective_id=0, has_side_effects=True, vmem_limit_bytes=40 << 20
         ),
-    )(layer_input[0, 0], keys[0, 0], values[0, 0], top_grad[0], gains, biases, lengths)
-    grad_in, key_grad, value_grad, gain_grad, bias_grad = outs
+    )(*[pltpu.with_memory_space_constraint(a, pltpu.HBM) for a in (layer_input[0, 0], keys[0, 0], values[0, 0], top_grad[0], gains, biases)], lengths)
+    grad_in, key_grad, value_grad, gain_grad, bias_grad = pl.pallas_call(
+        write,
+        out_shape=tuple(jax.ShapeDtypeStruct(out.shape, out.dtype) for out in outs),
+        in_specs=[vmem] * len(outs),
+        out_specs=(anywhere,) * len(outs),
+        scratch_shapes=[dma((len(outs),))],
+        compiler_params=pltpu.CompilerParams(vmem_limit_bytes=4 << 20),
+    )(*outs)
     return grad_in[None, None], key_grad[None, None], value_grad[None, None], gain_grad, bias_grad
 
 

time: 83.1 us -> 72.2 us (0.87)
  local copies, waits for them, and re-layouts: 9.08 us -> 0 us
  Pallas kernels: 72.3 us -> 70.8 us
    unnamed x17 -> x0, local copies, waits for them, and re-layouts: 9.08 us -> none
    pallas_call x1, Pallas kernels: 72.3 us -> 69.6 us  [local(): pl.pallas_call(functools.partial(kernel, sections), out_shape=(jax.ShapeD...]
    pallas_call x0 -> x1, Pallas kernels: none -> 1.18 us  [local(): pl.pallas_call(write, out_shape=tuple((jax.ShapeDtypeStruct(out.shape, ou...]
where the time goes in v2:
time: 72.2 us; the launch traced here: 72 us
  Pallas kernels  70.8 us (98%)
  between operations  1.29 us (2%)
    pallas_call x1, Pallas kernels, local(): pl.pallas_call(functools.partial(kernel, sections), out_shape=(jax.ShapeD...  69.6 us

profile of v2, /device:TPU:1, one launch (start us, length us, event | category | flops | bytes accessed | tf_op | source)
XLA Modules:
  0.0 72.0 jit_solution(12612219677642358636)
XLA Ops:
  1.3 69.6 %shard_map.110 = (bf16[128,4096]{1,0:T(8,128)(2,1)S(1)}, f32[128,512]{1,0:T(8,128)S(1)}, f32[128,512]{1,0:T(8,128)S(1)}, f32[1,64]{1,0:T(1,128)S(1)}, f32[1,64]{1,0:T(1,128)S(1)}) custom-call(bf16[128,4096]{1,0:T(8,128)(2,1)} %bitcast.7, bf16[128,512]{1,0:T(8,128)(2,1)} %bitcast.9, bf16[128,512]{1,0:T(8,128)(2,1)} %bitcast.10, bf16[128,4096]{1,0:T(8,128)(2,1)} %bitcast.8, ...), custom_call_target="tpu_custom_call" | custom-call | tf_op jit(solution)/shard_map/pallas_call | solution.py:381
  70.9 1.2 %shard_map.111 = (bf16[128,4096]{1,0:T(8,128)(2,1)}, f32[128,512]{1,0:T(8,128)}, f32[128,512]{1,0:T(8,128)}, f32[1,64]{1,0:T(1,128)}, f32[1,64]{1,0:T(1,128)}) custom-call(bf16[128,4096]{1,0:T(8,128)(2,1)S(1)} %get-tuple-element.15.refs_0_, f32[128,512]{1,0:T(8,128)S(1)} %get-tuple-element.16.refs_1_, f32[128,512]{1,0:T(8,128)S(1)} %get-tuple-element.17.refs_2_, ...), custom_call_target="tpu_custom_call" | custom-call | tf_op jit(solution)/shard_map/pallas_call | solution.py:435

commit v3 on v2

--- a/solution.py
+++ b/solution.py
@@ -21,6 +21,12 @@
 DP_X, DP_Z, DP_CORE = 4, 8, 2
 FACTOR = HD ** (-0.5)
 F32, BF16 = jnp.float32, jnp.bfloat16
+OFFSETS = sorted(
+    ((x, z, core) for x in range(DP_X) for z in range(DP_Z) for core in range(DP_CORE)),
+    key=lambda at: (-min(at[0], DP_X - at[0]) - min(at[1], DP_Z - at[1]), at),
+)
+OFFSETS.remove((0, 0, 0))
+PARTNERS = len(OFFSETS)
 
 
 def dot(a, b):
@@ -62,8 +68,8 @@
     keys, values, keys_t, values_t, gain_p, bias_p,
     arrived, sent, norm_p, inv_p, probs_p, mix_p, base_p,
     query_b, probs_b, grads_b, gain_acc, bias_acc,
-    first_src, first_dst, second_src, second_dst,
-    in_sem, x_sem, top_sem, send_sem, recv_sem, s1_send, s1_recv, s2_send, s2_recv,
+    share_src, share_dst,
+    in_sem, x_sem, top_sem, send_sem, recv_sem, share_sem,
 ):
     section = lax.axis_index("section")
     me = lax.axis_index("dp")
@@ -96,15 +102,13 @@
         for b in range(BLOCKS):
             top_copy(b).start()
 
-    def first_peer(k):
-        return {"dp": px * 16 + ((pz + k // 2) % 8) * 2 + (pc + k % 2) % 2}
-
-    def second_peer(k):
-        return {"dp": ((px + k // 2) % 4) * 16 + pz * 2 + (pc + k % 2) % 2}
+    def partner(k):
+        x, z, core = OFFSETS[k]
+        return ((px + x) % DP_X) * 16 + ((pz + z) % DP_Z) * 2 + (pc + core) % DP_CORE
 
     barrier = pltpu.get_barrier_semaphore()
     peers = [{"section": above}, {"section": below}]
-    peers += [first_peer(k) for k in range(1, 16)] + [second_peer(k) for k in range(2, 8)]
+    peers += [{"dp": partner(k)} for k in range(PARTNERS)]
     for peer in peers:
         pl.semaphore_signal(barrier, inc=1, device_id=peer, device_id_type=MESH)
 
@@ -218,9 +222,9 @@
         def _():
             hop(i).start()
 
-        @pl.when(held_back & (i % 2 == 1))
-        def _():
-            hop(i // 2).start()
+        @pl.when(held_back & ((2 * i) % 3 > 0))
+        def _():
+            hop((2 * i + 2) // 3 - 1).start()
 
         for p in range(2):
             grads_b[p, i] = kept[p]
@@ -263,38 +267,33 @@
             hop(i).start()
             return carry
 
-        lax.fori_loop(SPANS // 2, SPANS, late, 0)
-
-    for g, acc in enumerate((gain_acc, bias_acc)):
-        terms = acc[...].reshape(HALF, 8, HD)
-        halves = (jnp.sum(terms[:, :4], axis=1), jnp.sum(terms[:, 4:], axis=1))
-        for x in range(DP_X):
-            rows = halves[x // 2][(x % 2) * 8 : (x % 2) * 8 + 8]
-            for z in range(DP_Z):
-                first_src[g, z, x : x + 1, :] = rows[z : z + 1]
-
-    def first_copy(k):
+        lax.fori_loop(SPANS * 2 // 3, SPANS, late, 0)
+
+    left = lax.broadcasted_iota(jnp.int32, (HALF, HD), 1) < HD // 2
+    gain_terms, bias_terms = (acc[...].reshape(HALF, 8, HD) for acc in (gain_acc, bias_acc))
+    for j in range(2):
+        gain = jnp.sum(gain_terms[:, 4 * j : 4 * j + 4], axis=1)
+        bias = jnp.sum(bias_terms[:, 4 * j : 4 * j + 4], axis=1)
+        rows = (
+            jnp.where(left, gain, pltpu.roll(bias, HD // 2, 1)),
+            jnp.where(left, pltpu.roll(gain, HD // 2, 1), bias),
+        )
+        for h in range(HALF):
+            for core in range(DP_CORE):
+                share_src[2 * (HALF * j + h) + core] = rows[core][h : h + 1]
+
+    def share_copy(k):
         return pltpu.make_async_remote_copy(
-            src_ref=first_src.at[(pc + k % 2) % 2, (pz + k // 2) % 8],
-            dst_ref=first_dst.at[k],
-            send_sem=s1_send.at[k],
-            recv_sem=s1_recv.at[k],
-            device_id=first_peer(k),
+            src_ref=share_src.at[partner(k)],
+            dst_ref=share_dst.at[k],
+            send_sem=share_sem.at[0],
+            recv_sem=share_sem.at[1],
+            device_id={"dp": partner(k)},
             device_id_type=MESH,
         )
 
-    def second_copy(k):
-        return pltpu.make_async_remote_copy(
-            src_ref=second_src.at[(px + k // 2) % 4],
-            dst_ref=second_dst.at[k],
-            send_sem=s2_send.at[k],
-            recv_sem=s2_recv.at[k],
-            device_id=second_peer(k),
-            device_id_type=MESH,
-        )
-
-    for k in range(1, 16):
-        first_copy(k).start()
+    for k in range(PARTNERS):
+        share_copy(k).start()
 
     flat = SPANS * 64
 
@@ -307,15 +306,6 @@
         for j in range(2):
             head = p + 2 * j
             value_out[:, head * HD : (head + 1) * HD] = value_grad[j * SEQ : (j + 1) * SEQ]
-
-    total = first_src[pc, pz]
-    for k in range(1, 16):
-        first_copy(k).wait_recv()
-        total = total + first_dst[k]
-    for x in range(DP_X):
-        second_src[x] = total[x : x + 1]
-    for k in range(1, 8):
-        second_copy(k).start()
 
     for p in range(2):
         key_grad = contract(grads_b[p].reshape(flat, 2 * SEQ), query_b[p].reshape(flat, HD))
@@ -338,14 +328,10 @@
 
     lax.fori_loop(0, BLOCKS, unpack, 0)
 
-    shares = [second_src[px], jnp.zeros((1, HD), F32)]
-    for k in range(1, 8):
-        second_copy(k).wait_recv()
-        shares[k % 2] = shares[k % 2] + second_dst[k]
-    gain = jnp.where(pc == 0, shares[0], pltpu.roll(shares[1], HD // 2, 1))
-    bias = jnp.where(pc == 0, shares[1], pltpu.roll(shares[0], HD // 2, 1))
-    gain_out[...] = gain[:, : HD // 2]
-    bias_out[...] = bias[:, : HD // 2]
+    pltpu.make_async_copy(share_dst, share_dst, share_sem.at[1]).wait()
+    share = share_src[me] + jnp.sum(share_dst[...], axis=0)
+    gain_out[...] = share[:, : HD // 2]
+    bias_out[...] = pltpu.roll(share, HD // 2, 1)[:, : HD // 2]
 
     def sent_all(i, carry):
         hop(i).wait_send()
@@ -355,10 +341,7 @@
     def _():
         lax.fori_loop(0, SPANS, sent_all, 0)
 
-    for k in range(1, 16):
-        first_copy(k).wait_send()
-    for k in range(1, 8):
-        second_copy(k).wait_send()
+    pltpu.make_async_copy(share_dst, share_dst, share_sem.at[0]).wait()
 
 
 def write(*refs):
@@ -414,19 +397,14 @@
             pltpu.VMEM((2, SPANS, 64, 2 * SEQ), BF16),
             pltpu.VMEM((128, HD), F32),
             pltpu.VMEM((128, HD), F32),
-            pltpu.VMEM((DP_CORE, DP_Z, DP_X, HD), F32),
-            pltpu.VMEM((DP_Z * DP_CORE, DP_X, HD), F32),
-            pltpu.VMEM((DP_X, 1, HD), F32),
-            pltpu.VMEM((DP_X * DP_CORE, 1, HD), F32),
+            pltpu.VMEM((PARTNERS + 1, 1, HD), F32),
+            pltpu.VMEM((PARTNERS, 1, HD), F32),
             dma((4,)),
             dma((BLOCKS,)),
             dma((BLOCKS,)),
             dma((SPANS,)),
             dma((SPANS,)),
-            dma((16,)),
-            dma((16,)),
-            dma((8,)),
-            dma((8,)),
+            dma((2,)),
         ],
         compiler_params=pltpu.CompilerParams(
             collective_id=0, has_side_effects=True, vmem_limit_bytes=40 << 20

time: 72.2 us -> 69.5 us (0.963)
  Pallas kernels: 70.8 us -> 68.1 us
    pallas_call x1, Pallas kernels: 69.6 us -> 66.9 us  [local(): pl.pallas_call(functools.partial(kernel, sections), out_shape=(jax.ShapeD...]
where the time goes in v3:
time: 69.5 us; the launch traced here: 69.4 us
  Pallas kernels  68.1 us (98%)
  between operations  1.29 us (2%)
    pallas_call x1, Pallas kernels, local(): pl.pallas_call(functools.partial(kernel, sections), out_shape=(jax.ShapeD...  66.9 us

profile of v3, /device:TPU:1, one launch (start us, length us, event | category | flops | bytes accessed | tf_op | source)
XLA Modules:
  0.0 69.4 jit_solution(10651384164237276349)
XLA Ops:
  1.3 66.9 %shard_map.110 = (bf16[128,4096]{1,0:T(8,128)(2,1)S(1)}, f32[128,512]{1,0:T(8,128)S(1)}, f32[128,512]{1,0:T(8,128)S(1)}, f32[1,64]{1,0:T(1,128)S(1)}, f32[1,64]{1,0:T(1,128)S(1)}) custom-call(bf16[128,4096]{1,0:T(8,128)(2,1)} %bitcast.7, bf16[128,512]{1,0:T(8,128)(2,1)} %bitcast.9, bf16[128,512]{1,0:T(8,128)(2,1)} %bitcast.10, bf16[128,4096]{1,0:T(8,128)(2,1)} %bitcast.8, ...), custom_call_target="tpu_custom_call" | custom-call | tf_op jit(solution)/shard_map/pallas_call | solution.py:364
  68.2 1.2 %shard_map.111 = (bf16[128,4096]{1,0:T(8,128)(2,1)}, f32[128,512]{1,0:T(8,128)}, f32[128,512]{1,0:T(8,128)}, f32[1,64]{1,0:T(1,128)}, f32[1,64]{1,0:T(1,128)}) custom-call(bf16[128,4096]{1,0:T(8,128)(2,1)S(1)} %get-tuple-element.15.refs_0_, f32[128,512]{1,0:T(8,128)S(1)} %get-tuple-element.16.refs_1_, f32[128,512]{1,0:T(8,128)S(1)} %get-tuple-element.17.refs_2_, ...), custom_call_target="tpu_custom_call" | custom-call | tf_op jit(solution)/shard_map/pallas_call | solution.py:413

commit v4 on v3

--- a/solution.py
+++ b/solution.py
@@ -27,6 +27,13 @@
 )
 OFFSETS.remove((0, 0, 0))
 PARTNERS = len(OFFSETS)
+NEXT = ((0, 1, 0), (0, 7, 0), (1, 0, 0), (3, 0, 0), (0, 0, 1))
+ROUNDS = (
+    ((0, 1, 0), (0, 7, 0), (1, 0, 0), (3, 0, 0)),
+    ((0, 2, 0), (0, 6, 0)),
+    ((1, 0, 0), (3, 0, 0), (2, 0, 0)),
+    ((0, 0, 1),),
+)
 
 
 def dot(a, b):
@@ -69,7 +76,7 @@
     arrived, sent, norm_p, inv_p, probs_p, mix_p, base_p,
     query_b, probs_b, grads_b, gain_acc, bias_acc,
     share_src, share_dst,
-    in_sem, x_sem, top_sem, send_sem, recv_sem, share_sem,
+    in_sem, x_sem, top_sem, send_sem, recv_sem, share_sem, round_sem,
 ):
     section = lax.axis_index("section")
     me = lax.axis_index("dp")
@@ -106,9 +113,21 @@
         x, z, core = OFFSETS[k]
         return ((px + x) % DP_X) * 16 + ((pz + z) % DP_Z) * 2 + (pc + core) % DP_CORE
 
+    def place(x, z, core):
+        return {"dp": ((px + x) % DP_X) * 16 + ((pz + z) % DP_Z) * 2 + (pc + core) % DP_CORE}
+
+    def tell(r):
+        for x, z, core in ROUNDS[r]:
+            pl.semaphore_signal(
+                round_sem.at[r], inc=1, device_id=place(x, z, core), device_id_type=MESH
+            )
+
+    def hear(r):
+        pl.semaphore_wait(round_sem.at[r], len(ROUNDS[r]))
+
     barrier = pltpu.get_barrier_semaphore()
     peers = [{"section": above}, {"section": below}]
-    peers += [{"dp": partner(k)} for k in range(PARTNERS)]
+    peers += [place(x, z, core) for x, z, core in NEXT]
     for peer in peers:
         pl.semaphore_signal(barrier, inc=1, device_id=peer, device_id_type=MESH)
 
@@ -243,6 +262,7 @@
 
     prepare(0)
     pl.semaphore_wait(barrier, len(peers))
+    tell(0)
 
     def turn(t, carry):
         @pl.when(t >= lead)
@@ -256,6 +276,13 @@
         @pl.when(t + 1 < BLOCKS)
         def _():
             prepare(t + 1)
+
+        for r, at in enumerate((2, 4, 6)):
+
+            @pl.when(t == at)
+            def _(r=r):
+                hear(r)
+                tell(r + 1)
 
         return carry
 
@@ -292,6 +319,7 @@
             device_id_type=MESH,
         )
 
+    hear(len(ROUNDS) - 1)
     for k in range(PARTNERS):
         share_copy(k).start()
 
@@ -405,6 +433,7 @@
             dma((SPANS,)),
             dma((SPANS,)),
             dma((2,)),
+            pltpu.SemaphoreType.REGULAR((len(ROUNDS),)),
         ],
         compiler_params=pltpu.CompilerParams(
             collective_id=0, has_side_effects=True, vmem_limit_bytes=40 << 20

time: 69.5 us -> 68.1 us (0.980)
  Pallas kernels: 68.1 us -> 66.6 us
    pallas_call x1, Pallas kernels: 66.9 us -> 65.4 us  [local(): pl.pallas_call(functools.partial(kernel, sections), out_shape=(jax.ShapeD...]
where the time goes in v4:
time: 68.1 us; the launch traced here: 67.9 us
  Pallas kernels  66.6 us (98%)
  between operations  1.29 us (2%)
    pallas_call x1, Pallas kernels, local(): pl.pallas_call(functools.partial(kernel, sections), out_shape=(jax.ShapeD...  65.4 us

profile of v4, /device:TPU:1, one launch (start us, length us, event | category | flops | bytes accessed | tf_op | source)
XLA Modules:
  0.0 67.9 jit_solution(6683255291640193112)
XLA Ops:
  1.3 65.4 %shard_map.110 = (bf16[128,4096]{1,0:T(8,128)(2,1)S(1)}, f32[128,512]{1,0:T(8,128)S(1)}, f32[128,512]{1,0:T(8,128)S(1)}, f32[1,64]{1,0:T(1,128)S(1)}, f32[1,64]{1,0:T(1,128)S(1)}) custom-call(bf16[128,4096]{1,0:T(8,128)(2,1)} %bitcast.7, bf16[128,512]{1,0:T(8,128)(2,1)} %bitcast.9, bf16[128,512]{1,0:T(8,128)(2,1)} %bitcast.10, bf16[128,4096]{1,0:T(8,128)(2,1)} %bitcast.8, ...), custom_call_target="tpu_custom_call" | custom-call | tf_op jit(solution)/shard_map/pallas_call | solution.py:392
  66.7 1.2 %shard_map.111 = (bf16[128,4096]{1,0:T(8,128)(2,1)}, f32[128,512]{1,0:T(8,128)}, f32[128,512]{1,0:T(8,128)}, f32[1,64]{1,0:T(1,128)}, f32[1,64]{1,0:T(1,128)}) custom-call(bf16[128,4096]{1,0:T(8,128)(2,1)S(1)} %get-tuple-element.15.refs_0_, f32[128,512]{1,0:T(8,128)S(1)} %get-tuple-element.16.refs_1_, f32[128,512]{1,0:T(8,128)S(1)} %get-tuple-element.17.refs_2_, ...), custom_call_target="tpu_custom_call" | custom-call | tf_op jit(solution)/shard_map/pallas_call | solution.py:442

commit v5 on v4

--- a/solution.py
+++ b/solution.py
@@ -7,7 +7,7 @@
 from jax.experimental.pallas import tpu as pltpu
 from jax.sharding import PartitionSpec as P
 
-MESH = pl.DeviceIdType.MESH
+LOGICAL = pl.DeviceIdType.LOGICAL
 HD = 128
 KVH = 4
 SEQ = 128
@@ -17,6 +17,8 @@
 BLOCK = 16
 BLOCKS = SEQ // BLOCK
 PER_BLOCK = BLOCK // ROWS
+EARLY = 2
+GO = 26
 HALF = 16
 DP_X, DP_Z, DP_CORE = 4, 8, 2
 FACTOR = HD ** (-0.5)
@@ -76,7 +78,7 @@
     arrived, sent, norm_p, inv_p, probs_p, mix_p, base_p,
     query_b, probs_b, grads_b, gain_acc, bias_acc,
     share_src, share_dst,
-    in_sem, x_sem, top_sem, send_sem, recv_sem, share_sem, round_sem,
+    in_sem, x_sem, top_sem, send_sem, recv_sem, share_sem, round_sem, go_sem,
 ):
     section = lax.axis_index("section")
     me = lax.axis_index("dp")
@@ -114,22 +116,23 @@
         return ((px + x) % DP_X) * 16 + ((pz + z) % DP_Z) * 2 + (pc + core) % DP_CORE
 
     def place(x, z, core):
-        return {"dp": ((px + x) % DP_X) * 16 + ((pz + z) % DP_Z) * 2 + (pc + core) % DP_CORE}
+        dp = ((px + x) % DP_X) * 16 + ((pz + z) % DP_Z) * 2 + (pc + core) % DP_CORE
+        return dp * sections + section
 
     def tell(r):
         for x, z, core in ROUNDS[r]:
             pl.semaphore_signal(
-                round_sem.at[r], inc=1, device_id=place(x, z, core), device_id_type=MESH
+                round_sem.at[r], inc=1, device_id=place(x, z, core), device_id_type=LOGICAL
             )
 
     def hear(r):
         pl.semaphore_wait(round_sem.at[r], len(ROUNDS[r]))
 
     barrier = pltpu.get_barrier_semaphore()
-    peers = [{"section": above}, {"section": below}]
+    peers = [me * sections + above, me * sections + below]
     peers += [place(x, z, core) for x, z, core in NEXT]
     for peer in peers:
-        pl.semaphore_signal(barrier, inc=1, device_id=peer, device_id_type=MESH)
+        pl.semaphore_signal(barrier, inc=1, device_id=peer, device_id_type=LOGICAL)
 
     low8, low64, low128 = low_of(8), low_of(64), low_of(128)
     for copy in small:
@@ -158,6 +161,7 @@
         normed = inputs * inverse
         inverse = jnp.broadcast_to(inverse, (BLOCK, HD))
         gains, biases = gain_p[...], bias_p[...]
+        items = []
         for half in range(2):
             rows = slice(half * 8, half * 8 + 8)
             pair = pack(normed[rows], low8)
@@ -172,27 +176,34 @@
                 gained = norm * gains
                 query = (gained + biases).astype(BF16)
                 gained = gained.astype(BF16)
-                position = span * ROWS + offsets
-                live = tiled(jnp.where(position < length, 1.0, 0.0).astype(F32), 8)
-                allowed = tiled(
-                    jnp.where((columns <= position) & (columns < length), 1.0, 0.0).astype(F32), 8
-                )
                 for p in range(2):
                     part = slice(64 * p, 64 * p + 64)
-                    query_b[p, span] = query[part]
-                    both = dot(jnp.concatenate([query[part], gained[part]], axis=0), keys_t[p])
-                    both = pick(both, low128)
-                    scores = jnp.where(allowed > 0.5, both[:64] * FACTOR, -1e30)
-                    mix_p[span, part, :] = both[64:]
-                    weights = jnp.exp(scores - jnp.max(scores, -1, keepdims=True))
-                    weights = weights * (1.0 / jnp.sum(weights, -1, keepdims=True)) * live
-                    probs_p[span, part, :] = weights * FACTOR
-                    wide = spread(weights, low64)
-                    high = wide.astype(BF16)
-                    probs_b[p, span] = high
-                    rest = (wide - high.astype(F32)).astype(BF16)
-                    outs = dot(jnp.concatenate([high, rest], axis=0), values[p])
-                    base_p[span, part, :] = outs[:64] + outs[64:]
+                    items.append((span, p, part, query[part], gained[part]))
+        boths = [
+            pick(dot(jnp.concatenate([query, gained], axis=0), keys_t[p]), low128)
+            for _, p, _, query, gained in items
+        ]
+        results = []
+        for (span, p, part, _, _), both in zip(items, boths):
+            position = span * ROWS + offsets
+            live = tiled(jnp.where(position < length, 1.0, 0.0).astype(F32), 8)
+            allowed = tiled(
+                jnp.where((columns <= position) & (columns < length), 1.0, 0.0).astype(F32), 8
+            )
+            scores = jnp.where(allowed > 0.5, both[:64] * FACTOR, -1e30)
+            weights = jnp.exp(scores - jnp.max(scores, -1, keepdims=True))
+            weights = weights * (1.0 / jnp.sum(weights, -1, keepdims=True)) * live
+            wide = spread(weights, low64)
+            high = wide.astype(BF16)
+            rest = (wide - high.astype(F32)).astype(BF16)
+            outs = dot(jnp.concatenate([high, rest], axis=0), values[p])
+            results.append((weights, high, outs))
+        for (span, p, part, query, _), both, (weights, high, outs) in zip(items, boths, results):
+            query_b[p, span] = query
+            mix_p[span, part, :] = both[64:]
+            probs_p[span, part, :] = weights * FACTOR
+            probs_b[p, span] = high
+            base_p[span, part, :] = outs[:64] + outs[64:]
 
     def take_top(b):
         top_copy(b).wait()
@@ -208,47 +219,49 @@
             dst_ref=arrived.at[i],
             send_sem=send_sem.at[i],
             recv_sem=recv_sem.at[i],
-            device_id={"section": below},
-            device_id_type=MESH,
+            device_id=me * sections + below,
+            device_id_type=LOGICAL,
         )
 
-    def backward(i):
-        @pl.when(jnp.logical_not(is_top))
-        def _():
-            hop(i).wait_recv()
-
-        upstream = arrived[i]
-        wide = upstream.astype(F32)
-        centre = jnp.sum(wide * base_p[i], -1, keepdims=True)
-        queries, kept, totals = [], [], jnp.zeros((8, HD), F32)
+    def backward(spans):
+        upstreams = [arrived[i] for i in spans]
+        wides = [upstream.astype(F32) for upstream in upstreams]
+        centres = [jnp.sum(wide * base_p[i], -1, keepdims=True) for i, wide in zip(spans, wides)]
+        totals = [jnp.zeros((8, HD), F32) for _ in spans]
+        kept, queries = [[] for _ in spans], [[] for _ in spans]
         for p in range(2):
             part = slice(64 * p, 64 * p + 64)
-            grad_probs = pick(dot(upstream[part], values_t[p]), low64)
-            grads = probs_p[i, part, :] * (grad_probs - centre[part])
-            totals = totals + jnp.sum((grads * mix_p[i, part, :]).reshape(8, 8, HD), axis=0)
-            grads_wide = spread(grads, low64).astype(BF16)
-            kept.append(grads_wide)
-            queries.append(dot(grads_wide, keys[p]))
-        mean = jnp.sum(totals, -1, keepdims=True) * (1.0 / WIDTH)
-        mean = jnp.broadcast_to(mean, (8, HD))
-        mean = mean + pltpu.roll(mean, 4, 0)
-        grad_query = jnp.concatenate(queries, axis=0)
-        norm = norm_p[i]
-        change = grad_query * gain_p[...] - norm * tiled(mean, HALF)
-        sent[i] = (wide + tiled(inv_p[i], HALF) * change).astype(BF16)
-
-        @pl.when((section > 0) & jnp.logical_not(held_back))
-        def _():
-            hop(i).start()
-
-        @pl.when(held_back & ((2 * i) % 3 > 0))
-        def _():
-            hop((2 * i + 2) // 3 - 1).start()
-
+            for n, i in enumerate(spans):
+                grad_probs = pick(dot(upstreams[n][part], values_t[p]), low64)
+                grads = probs_p[i, part, :] * (grad_probs - centres[n][part])
+                mixed = (grads * mix_p[i, part, :]).reshape(8, 8, HD)
+                totals[n] = totals[n] + jnp.sum(mixed, axis=0)
+                kept[n].append(spread(grads, low64).astype(BF16))
         for p in range(2):
-            grads_b[p, i] = kept[p]
-        gain_acc[...] += grad_query * norm
-        bias_acc[...] += grad_query
+            for n in range(len(spans)):
+                queries[n].append(dot(kept[n][p], keys[p]))
+        rest = []
+        for n, i in enumerate(spans):
+            mean = jnp.sum(totals[n], -1, keepdims=True) * (1.0 / WIDTH)
+            mean = jnp.broadcast_to(mean, (8, HD))
+            mean = mean + pltpu.roll(mean, 4, 0)
+            grad_query = jnp.concatenate(queries[n], axis=0)
+            norm = norm_p[i]
+            change = grad_query * gain_p[...] - norm * tiled(mean, HALF)
+            sent[i] = (wides[n] + tiled(inv_p[i], HALF) * change).astype(BF16)
+            rest.append((i, kept[n], grad_query, norm))
+        return rest
+
+    def finish(rest):
+        gains = biases = None
+        for i, kept, grad_query, norm in rest:
+            for p in range(2):
+                grads_b[p, i] = kept[p]
+            gained = grad_query * norm
+            gains = gained if gains is None else gains + gained
+            biases = grad_query if biases is None else biases + grad_query
+        gain_acc[...] += gains
+        bias_acc[...] += biases
 
     behind = sections - 1 - section
     lead = jnp.where(behind == 0, 0, jnp.where(behind == 1, 3, jnp.where(behind == 2, 6, BLOCKS - 1)))
@@ -265,10 +278,35 @@
     tell(0)
 
     def turn(t, carry):
-        @pl.when(t >= lead)
+        @pl.when(is_top)
+        def _():
+            first = t * PER_BLOCK
+            rest = backward([first + q for q in range(PER_BLOCK)])
+
+            @pl.when(pc == 0)
+            def _():
+                for q in range(PER_BLOCK):
+                    hop(first + q).start()
+
+            @pl.when(pc == 1)
+            def _():
+                for q in range(EARLY):
+                    hop(t * EARLY + q).start()
+
+            finish(rest)
+
+        @pl.when((t >= lead) & jnp.logical_not(is_top))
         def _():
             def step(q, c):
-                backward((t - lead) * PER_BLOCK + q)
+                i = (t - lead) * PER_BLOCK + q
+                hop(i).wait_recv()
+                rest = backward([i])
+
+                @pl.when(section > 0)
+                def _():
+                    hop(i).start()
+
+                finish(rest)
                 return c
 
             lax.fori_loop(0, PER_BLOCK, step, 0)
@@ -287,6 +325,17 @@
         return carry
 
     lax.fori_loop(0, BLOCKS + lead, turn, 0)
+
+    def sent_some(i, carry):
+        hop(i).wait_send()
+        return carry
+
+    leader = is_top & (pc == 0)
+
+    @pl.when(leader)
+    def _():
+        lax.fori_loop(0, GO, sent_some, 0)
+        pl.semaphore_signal(go_sem, inc=1, device_id=place(0, 0, 1), device_id_type=LOGICAL)
 
     @pl.when(held_back)
     def _():
@@ -294,7 +343,8 @@
             hop(i).start()
             return carry
 
-        lax.fori_loop(SPANS * 2 // 3, SPANS, late, 0)
+        pl.semaphore_wait(go_sem, 1)
+        lax.fori_loop(BLOCKS * EARLY, SPANS, late, 0)
 
     left = lax.broadcasted_iota(jnp.int32, (HALF, HD), 1) < HD // 2
     gain_terms, bias_terms = (acc[...].reshape(HALF, 8, HD) for acc in (gain_acc, bias_acc))
@@ -315,8 +365,8 @@
             dst_ref=share_dst.at[k],
             send_sem=share_sem.at[0],
             recv_sem=share_sem.at[1],
-            device_id={"dp": partner(k)},
-            device_id_type=MESH,
+            device_id=partner(k) * sections + section,
+            device_id_type=LOGICAL,
         )
 
     hear(len(ROUNDS) - 1)
@@ -361,13 +411,9 @@
     gain_out[...] = share[:, : HD // 2]
     bias_out[...] = pltpu.roll(share, HD // 2, 1)[:, : HD // 2]
 
-    def sent_all(i, carry):
-        hop(i).wait_send()
-        return carry
-
     @pl.when(section > 0)
     def _():
-        lax.fori_loop(0, SPANS, sent_all, 0)
+        lax.fori_loop(jnp.where(leader, GO, 0), SPANS, sent_some, 0)
 
     pltpu.make_async_copy(share_dst, share_dst, share_sem.at[0]).wait()
 
@@ -434,6 +480,7 @@
             dma((SPANS,)),
             dma((2,)),
             pltpu.SemaphoreType.REGULAR((len(ROUNDS),)),
+            pltpu.SemaphoreType.REGULAR,
         ],
         compiler_params=pltpu.CompilerParams(
             collective_id=0, has_side_effects=True, vmem_limit_bytes=40 << 20

time: 68.1 us -> 67.8 us (level)
  no operation moved by 1% of the time
where the time goes in v5:
time: 67.8 us; the launch traced here: 67.6 us
  Pallas kernels  66.4 us (98%)
  between operations  1.29 us (2%)
    pallas_call x1, Pallas kernels, local(): pl.pallas_call(functools.partial(kernel, sections), out_shape=(jax.ShapeD...  65.2 us

profile of v5, /device:TPU:1, one launch (start us, length us, event | category | flops | bytes accessed | tf_op | source)
XLA Modules:
  0.0 67.6 jit_solution(11993507646961251092)
XLA Ops:
  1.3 65.2 %shard_map.110 = (bf16[128,4096]{1,0:T(8,128)(2,1)S(1)}, f32[128,512]{1,0:T(8,128)S(1)}, f32[128,512]{1,0:T(8,128)S(1)}, f32[1,64]{1,0:T(1,128)S(1)}, f32[1,64]{1,0:T(1,128)S(1)}) custom-call(bf16[128,4096]{1,0:T(8,128)(2,1)} %bitcast.7, bf16[128,512]{1,0:T(8,128)(2,1)} %bitcast.9, bf16[128,512]{1,0:T(8,128)(2,1)} %bitcast.10, bf16[128,4096]{1,0:T(8,128)(2,1)} %bitcast.8, ...), custom_call_target="tpu_custom_call" | custom-call | tf_op jit(solution)/shard_map/pallas_call | solution.py:438
  66.5 1.2 %shard_map.111 = (bf16[128,4096]{1,0:T(8,128)(2,1)}, f32[128,512]{1,0:T(8,128)}, f32[128,512]{1,0:T(8,128)}, f32[1,64]{1,0:T(1,128)}, f32[1,64]{1,0:T(1,128)}) custom-call(bf16[128,4096]{1,0:T(8,128)(2,1)S(1)} %get-tuple-element.15.refs_0_, f32[128,512]{1,0:T(8,128)S(1)} %get-tuple-element.16.refs_1_, f32[128,512]{1,0:T(8,128)S(1)} %get-tuple-element.17.refs_2_, ...), custom_call_target="tpu_custom_call" | custom-call | tf_op jit(solution)/shard_map/pallas_call | solution.py:489

commit v6 on v5

--- a/solution.py
+++ b/solution.py
@@ -19,6 +19,7 @@
 PER_BLOCK = BLOCK // ROWS
 EARLY = 2
 GO = 26
+PARTS = 4
 HALF = 16
 DP_X, DP_Z, DP_CORE = 4, 8, 2
 FACTOR = HD ** (-0.5)
@@ -420,8 +421,12 @@
 
 def write(*refs):
     count = len(refs) // 2
+    pairs = [(refs[i], refs[count + i]) for i in range(1, count)]
+    for part in range(PARTS):
+        rows = pl.ds(part * (SEQ // PARTS), SEQ // PARTS)
+        pairs.append((refs[0].at[rows], refs[count].at[rows]))
     copies = [
-        pltpu.make_async_copy(refs[i], refs[count + i], refs[-1].at[i]) for i in range(count)
+        pltpu.make_async_copy(src, dst, refs[-1].at[i]) for i, (src, dst) in enumerate(pairs)
     ]
     for copy in copies:
         copy.start()
@@ -491,7 +496,7 @@
         out_shape=tuple(jax.ShapeDtypeStruct(out.shape, out.dtype) for out in outs),
         in_specs=[vmem] * len(outs),
         out_specs=(anywhere,) * len(outs),
-        scratch_shapes=[dma((len(outs),))],
+        scratch_shapes=[dma((len(outs) - 1 + PARTS,))],
         compiler_params=pltpu.CompilerParams(vmem_limit_bytes=4 << 20),
     )(*outs)
     return grad_in[None, None], key_grad[None, None], value_grad[None, None], gain_grad, bias_grad

time: 67.8 us -> 67.8 us (level)
  no operation moved by 1% of the time
where the time goes in v6:
time: 67.8 us; the launch traced here: 67.7 us
  Pallas kernels  66.4 us (98%)
  between operations  1.29 us (2%)
    pallas_call x1, Pallas kernels, local(): pl.pallas_call(functools.partial(kernel, sections), out_shape=(jax.ShapeD...  65.2 us

profile of v6, /device:TPU:1, one launch (start us, length us, event | category | flops | bytes accessed | tf_op | source)
XLA Modules:
  0.0 67.7 jit_solution(3520046523692593596)
XLA Ops:
  1.3 65.2 %shard_map.110 = (bf16[128,4096]{1,0:T(8,128)(2,1)S(1)}, f32[128,512]{1,0:T(8,128)S(1)}, f32[128,512]{1,0:T(8,128)S(1)}, f32[1,64]{1,0:T(1,128)S(1)}, f32[1,64]{1,0:T(1,128)S(1)}) custom-call(bf16[128,4096]{1,0:T(8,128)(2,1)} %bitcast.7, bf16[128,512]{1,0:T(8,128)(2,1)} %bitcast.9, bf16[128,512]{1,0:T(8,128)(2,1)} %bitcast.10, bf16[128,4096]{1,0:T(8,128)(2,1)} %bitcast.8, ...), custom_call_target="tpu_custom_call" | custom-call | tf_op jit(solution)/shard_map/pallas_call | solution.py:443
  66.5 1.2 %shard_map.111 = (bf16[128,4096]{1,0:T(8,128)(2,1)}, f32[128,512]{1,0:T(8,128)}, f32[128,512]{1,0:T(8,128)}, f32[1,64]{1,0:T(1,128)}, f32[1,64]{1,0:T(1,128)}) custom-call(bf16[128,4096]{1,0:T(8,128)(2,1)S(1)} %get-tuple-element.15.refs_0_, f32[128,512]{1,0:T(8,128)S(1)} %get-tuple-element.16.refs_1_, f32[128,512]{1,0:T(8,128)S(1)} %get-tuple-element.17.refs_2_, ...), custom_call_target="tpu_custom_call" | custom-call | tf_op jit(solution)/shard_map/pallas_call | solution.py:494
